TPU v7x, 32 devices: a whole 2x2x4 slice. The times are simulated.
32 devices in a mesh: fus: 8 (over z, x), blade: 4 (over y, core).
Axes of the slice: x: 2, y: 2, z: 4, core: 2. Of those that a mesh axis runs over, the one named last changes fastest.
Arguments:
- airframe_coords: float32 [3, 2048], P(None, 'fus'), may hold values from -6 to 6
- airframe_normals: float32 [3, 2048], P(None, 'fus'), may hold values from -6 to 6
- airframe_strength: float32 [4, 2048], P(None, 'fus'), may hold values from -6 to 6
- blade_coords: float32 [4, 3, 16384], P(None, None, ('fus', 'blade')), may hold values from -6 to 6
- blade_strength: float32 [4, 16384], P(None, ('fus', 'blade')), may hold values from -6 to 6
- blade_index: int32 [16384], P(('fus', 'blade')), may hold values from 0 to 3
- azimuth: float32 [4], replicated, may hold values from -3.140625 to 3.140625
- onset: float32 [3], replicated, may hold values from -4 to 4
Outputs:
- normal_velocity: float32 [4, 2048], P(None, ('fus', 'blade'))
- blade_velocity: float32 [4, 3, 16384], P(None, None, ('fus', 'blade'))
- residual: float32 [4, 2048], P(None, ('fus', 'blade'))
All inputs are finite; a program needn't handle non-finite values.
Results may differ from a plain program's by a relative error of at most 0.0001.
Values sent between devices are 32-bit elements; how exact they have to be, the bound alone decides.
A program may use at most 64 MiB of HBM per device.

v0:
```python
import math

import jax
import jax.numpy as jnp
from jax import lax
from jax.sharding import PartitionSpec as P

core_sq = 0.01
kernel_scale = 1.0 / (4.0 * math.pi)


def rotate(blade_coords, blade_index, azimuth):
    angle = azimuth[:, None] + blade_index.astype(jnp.float32)[None, :] * (math.pi / 2.0)
    cosine = jnp.cos(angle)
    sine = jnp.sin(angle)
    return jnp.stack(
        [
            cosine * blade_coords[:, 0] - sine * blade_coords[:, 1],
            sine * blade_coords[:, 0] + cosine * blade_coords[:, 1],
            blade_coords[:, 2],
        ],
        axis=1,
    )


def tile_terms(frame_pos, frame_norm, frame_str, blade_pos, blade_str):
    delta_x = frame_pos[0][:, None] - blade_pos[0][None, :]
    delta_y = frame_pos[1][:, None] - blade_pos[1][None, :]
    delta_z = frame_pos[2][:, None] - blade_pos[2][None, :]
    dist_sq = delta_x * delta_x + delta_y * delta_y + delta_z * delta_z + core_sq
    weight = kernel_scale * lax.rsqrt(dist_sq) / dist_sq
    projected = (
        frame_norm[0][:, None] * delta_x
        + frame_norm[1][:, None] * delta_y
        + frame_norm[2][:, None] * delta_z
    )
    normal_term = jnp.sum(weight * projected * blade_str[None, :], axis=1)
    scaled = weight * frame_str[:, None]
    blade_term = -jnp.stack(
        [jnp.sum(scaled * delta_x, 0), jnp.sum(scaled * delta_y, 0), jnp.sum(scaled * delta_z, 0)]
    )
    return (normal_term, blade_term)


def all_substeps(frame_pos, frame_norm, frame_str, blade_pos, blade_str):
    mapped = jax.vmap(tile_terms, in_axes=(None, None, 0, 0, 0))
    return mapped(frame_pos, frame_norm, frame_str, blade_pos, blade_str)


def blade_blocks(frame_pos, frame_norm, frame_str, piece):
    substeps = piece.shape[0]
    width = piece.shape[2]
    block = math.gcd(width, 1024)
    count = width // block
    pieces = jnp.transpose(piece.reshape(substeps, 4, count, block), (2, 0, 1, 3))

    def step_fn(carry, part):
        normal_term, blade_term = all_substeps(
            frame_pos, frame_norm, frame_str, part[:, :3], part[:, 3]
        )
        return (carry + normal_term, blade_term)

    normal_sum, blade_terms = lax.scan(
        step_fn, jnp.zeros((substeps, frame_pos.shape[1]), jnp.float32), pieces
    )
    return (normal_sum, jnp.transpose(blade_terms, (1, 2, 0, 3)).reshape(substeps, 3, width))


def body(
    airframe_coords,
    airframe_normals,
    airframe_strength,
    blade_coords,
    blade_strength,
    blade_index,
    azimuth,
    onset,
):
    b_rows = blade_strength.shape[1]
    rotated = rotate(blade_coords, blade_index, azimuth)
    packed = jnp.concatenate([rotated, blade_strength[:, None, :]], axis=1)
    normal_term, blade_term = blade_blocks(
        airframe_coords,
        airframe_normals,
        airframe_strength,
        lax.all_gather(packed, "fus", axis=2, tiled=True),
    )
    totals = lax.psum(blade_term, "fus")
    blade_velocity = lax.dynamic_slice_in_dim(totals, lax.axis_index("fus") * b_rows, b_rows, 2)
    normal_velocity = lax.psum_scatter(normal_term, "blade", scatter_dimension=1, tiled=True)
    quarter = normal_velocity.shape[1]
    offset = lax.axis_index("blade") * quarter
    own_normals = lax.dynamic_slice_in_dim(airframe_normals, offset, quarter, 1)
    own_strength = lax.dynamic_slice_in_dim(airframe_strength, offset, quarter, 1)
    onset_part = own_normals[0] * onset[0] + own_normals[1] * onset[1] + own_normals[2] * onset[2]
    residual = normal_velocity + onset_part[None, :] + 0.5 * own_strength
    return (normal_velocity, blade_velocity, residual)


def solution(mesh):
    placed = (
        P(None, "fus"),
        P(None, "fus"),
        P(None, "fus"),
        P(None, None, ("fus", "blade")),
        P(None, ("fus", "blade")),
        P(("fus", "blade")),
        P(),
        P(),
    )
    return jax.shard_map(
        body,
        mesh=mesh,
        in_specs=placed,
        out_specs=(
            P(None, ("fus", "blade")),
            P(None, None, ("fus", "blade")),
            P(None, ("fus", "blade")),
        ),
        check_vma=False,
    )
```

profile of v0, /device:TPU:0, one launch (start us, length us, event | category | flops | bytes accessed | tf_op | source)
XLA Modules:
  0.0 147.7 jit_solution(13118012814194301455)
XLA Ops:
  8.0 0.0 reduce-scatter.4.cloned.1.call-start
  8.1 0.7 convert_multiply_fusion
  8.7 0.9 fusion.17
  9.6 0.7 pad_maximum_fusion
  10.3 32.5 %all_gather.3 = f32[4,4,4096]{2,0,1:T(4,128)S(1)} all-gather(f32[4,4,512]{2,0,1:T(4,128)S(1)} %pad_maximum_fusion), channel_id=1, replica_groups=mesh['fus'=8,'blade'=4] {'fus'}, dimensions={2}, use_global_device_ids=true | all-gather | bytes 294912 | tf_op jit(solution)/shard_map/all_gather | solution.py:86
  42.9 0.2 reshape.101
  43.1 0.5 copy-done
  43.5 0.0 copy-done.1
  43.6 0.0 copy-done.4
  43.6 19.7 %while.13 = (s32[]{:T(128)}, f32[4,256]{1,0:T(4,128)S(1)}, f32[4,4,3,1024]{3,1,2,0:T(4,128)S(1)}, f32[3,256]{1,0:T(4,128)S(1)}, f32[4,4,4,1024]{3,0,1,2:T(4,128)...) while((s32[]{:T(128)}, f32[4,256]{1,0:T(4,128)S(1)}, ...), condition=%wide.region_5.6_spmd.clone, body=%wide.region_0.5_spmd.clone.sunk | while | flops 27288576 | bytes 645231 | solution.py:63
  43.6 0.1 constant_dynamic-slice_fusion.4
  43.7 4.7 %fusion.26 = (f32[4,1024]{1,0:T(4,128)S(1)}, f32[4,1024]{1,0:T(4,128)S(1)}, f32[4,1024]{1,0:T(4,128)S(1)}, f32[4,256]{1,0:T(4,128)S(1)}) fusion(f32[4,256]{1,0:T(4,128)S(1)} %get-tuple-element.220, f32[4,1024]{1,0:T(4,128)S(1)} %get-tuple-element.182, f32[256]{0:T(256)S(1)} %bitcast.77, f32[4,1024]{1,0:T(4,128)S(1)} %get-tuple-element.184, ...), kind=kLoop, calls=%fused_computation.17.clone.1 | loop fusion | flops 27249664 | bytes 129024 | tf_op jit(solution)/shard_map/while/body/eval_jaxpr/vmap()/reduce_sum | solution.py:40
  48.5 0.1 constant_dynamic-slice_fusion.4
  48.6 4.7 %fusion.26 = (f32[4,1024]{1,0:T(4,128)S(1)}, f32[4,1024]{1,0:T(4,128)S(1)}, f32[4,1024]{1,0:T(4,128)S(1)}, f32[4,256]{1,0:T(4,128)S(1)}) fusion(f32[4,256]{1,0:T(4,128)S(1)} %get-tuple-element.220, f32[4,1024]{1,0:T(4,128)S(1)} %get-tuple-element.182, f32[256]{0:T(256)S(1)} %bitcast.77, f32[4,1024]{1,0:T(4,128)S(1)} %get-tuple-element.184, ...), kind=kLoop, calls=%fused_computation.17.clone.1 | loop fusion | flops 27249664 | bytes 129024 | tf_op jit(solution)/shard_map/while/body/eval_jaxpr/vmap()/reduce_sum | solution.py:40
  53.4 0.1 constant_dynamic-slice_fusion.4
  53.5 4.7 %fusion.26 = (f32[4,1024]{1,0:T(4,128)S(1)}, f32[4,1024]{1,0:T(4,128)S(1)}, f32[4,1024]{1,0:T(4,128)S(1)}, f32[4,256]{1,0:T(4,128)S(1)}) fusion(f32[4,256]{1,0:T(4,128)S(1)} %get-tuple-element.220, f32[4,1024]{1,0:T(4,128)S(1)} %get-tuple-element.182, f32[256]{0:T(256)S(1)} %bitcast.77, f32[4,1024]{1,0:T(4,128)S(1)} %get-tuple-element.184, ...), kind=kLoop, calls=%fused_computation.17.clone.1 | loop fusion | flops 27249664 | bytes 129024 | tf_op jit(solution)/shard_map/while/body/eval_jaxpr/vmap()/reduce_sum | solution.py:40
  58.3 0.1 constant_dynamic-slice_fusion.4
  58.5 4.7 %fusion.26 = (f32[4,1024]{1,0:T(4,128)S(1)}, f32[4,1024]{1,0:T(4,128)S(1)}, f32[4,1024]{1,0:T(4,128)S(1)}, f32[4,256]{1,0:T(4,128)S(1)}) fusion(f32[4,256]{1,0:T(4,128)S(1)} %get-tuple-element.220, f32[4,1024]{1,0:T(4,128)S(1)} %get-tuple-element.182, f32[256]{0:T(256)S(1)} %bitcast.77, f32[4,1024]{1,0:T(4,128)S(1)} %get-tuple-element.184, ...), kind=kLoop, calls=%fused_computation.17.clone.1 | loop fusion | flops 27249664 | bytes 129024 | tf_op jit(solution)/shard_map/while/body/eval_jaxpr/vmap()/reduce_sum | solution.py:40
  63.2 0.8 copy.21
  64.0 0.0 reduce-scatter.4.cloned.1.call-update
  64.1 0.0 all-reduce.2.cloned.1.call-start
  64.1 0.0 copy-start.3
  64.1 0.7 copy.26
  64.8 0.0 all-reduce.2.cloned.1.call-update
  64.8 0.1 constant_dynamic-slice_fusion.1
  64.9 0.6 fusion.21
  65.5 1.9 %add_bitcast_fusion = f32[64]{0:T(128)S(1)} fusion(f32[3,64]{1,0:T(4,128)S(1)} %constant_dynamic-slice_fusion.1, f32[]{:T(128)} %bitcast.8, f32[]{:T(128)} %bitcast.7, f32[]{:T(128)} %bitcast.6), kind=kLoop, calls=%fused_computation.44 | loop fusion | flops 320 | bytes 1036 | tf_op jit(solution)/shard_map/add | solution.py:96
  67.5 17.3 %reduce-scatter.4.cloned.1.call-done = f32[64,4]{1,0:T(8,128)} async-done(((f32[256,4]{1,0:T(8,128)}), f32[64,4]{1,0:T(8,128)}) %reduce-scatter.4.cloned.1.call-update) | async-done | bytes 1040
  84.8 0.8 copy.22
  85.6 0.7 multiply_add_fusion
  86.3 52.6 %all-reduce.2.cloned.1.call-done = f32[4,3,4096]{2,0,1:T(4,128)} async-done(((f32[4,3,4096]{2,0,1:T(4,128)}), f32[4,3,4096]{2,0,1:T(4,128)}) %all-reduce.2.cloned.1.call-update) | async-done | bytes 196624 | tf_op jit(solution)/shard_map/psum | solution.py:88
  138.9 1.3 constant_dynamic-slice_fusion.2
  (28 shorter events, 0.3 us)
Async XLA Ops:
  8.0 76.8 %reduce-scatter.4.cloned.1.call-start = ((), (), s32[]{:S(2)}) async-start(), calls=%async_computation.2 | async-start | bytes 163840
  42.8 0.7 copy-start
  42.9 0.7 copy-start.1
  42.9 0.7 copy-start.4
  64.1 74.9 %all-reduce.2.cloned.1.call-start = ((), (), s32[]{:S(2)}) async-start(), calls=%async_computation.1 | async-start | bytes 393216 | tf_op jit(solution)/shard_map/psum | solution.py:88
  64.1 0.8 copy-start.3
  85.6 54.6 %copy-start.2 = (f32[4,64]{1,0:T(4,128)}, f32[4,64]{1,0:T(4,128)S(1)}, u32[]{:S(2)}) copy-start(f32[4,64]{1,0:T(4,128)S(1)} %copy.22) | copy-start | bytes 3076
Sparse Core Ops, SparseCore 0:
  64.2 20.5 reduce-scatter.3
Sparse Core Ops, SparseCore 1:
  68.2 70.7 all-reduce.1
where the time goes:
time: 148 us
  waiting for transfers between devices  70 us (47%)
  blocking collectives  32.5 us (22%)
  other arithmetic  23.9 us (16%)
  between operations  15.5 us (10%)
  local copies, waits for them, and re-layouts  5.46 us (4%)
    psum x1, waiting for transfers between devices, body(): totals = lax.psum(blade_term, 'fus')  52.6 us
    all_gather x1, blocking collectives, body(): lax.all_gather(packed, 'fus', axis=2, tiled=True)  32.5 us
    reduce_sum x4, other arithmetic, tile_terms(): jnp.sum(scaled * delta_x, 0)  18.9 us
    unnamed x3, waiting for transfers between devices  17.4 us
  transfers between devices with their start and end apart: 2, of which 2 were waited for; matrix products, arithmetic and copies ran while one was open for 3% of the time, Pallas kernels for 0%

commit v1 on v0

v1 whole, which is shorter than its diff:
```python
import functools
import math

import jax
import jax.numpy as jnp
from jax import lax
from jax.experimental import pallas as pl
from jax.experimental.pallas import tpu as pltpu
from jax.sharding import PartitionSpec as P

core_sq = 0.01
kernel_scale = 1.0 / (4.0 * math.pi)
MESH = pl.DeviceIdType.MESH
F32 = jnp.float32
BF16 = jnp.bfloat16
LANES = 128
ROWS = 16


def split3(value):
    high = value.astype(BF16).astype(F32)
    rest = value - high
    mid = rest.astype(BF16).astype(F32)
    low = (rest - mid).astype(BF16).astype(F32)
    return jnp.concatenate([high, mid, low, jnp.zeros_like(value)], axis=0).astype(BF16)


def fold3(parts):
    pair = parts[0:8] + parts[8:16]
    return pair[0:4] + pair[4:8]


def kernel(
    n, nb,
    ac_ref, an_ref, aq_ref, bc_ref, bs_ref, bi_ref, az_ref, on_ref,
    nv_ref, bv_ref, rs_ref,
    gath, spread, pos, yparts, xparts, whi, wlo, acc, stage, land,
    g_send, g_recv, p_send, p_recv,
):
    steps = bc_ref.shape[0]
    width = bc_ref.shape[2]
    frame = ac_ref.shape[1]
    quarter = frame // nb
    per_chunk = LANES // quarter
    me_f = lax.axis_index("fus")
    me_b = lax.axis_index("blade")

    barrier = pltpu.get_barrier_semaphore()

    def greet(i, _):
        other = lax.rem(me_f * nb + me_b + i, n * nb)
        pl.semaphore_signal(
            barrier, inc=1, device_id=(other // nb, lax.rem(other, nb)), device_id_type=MESH
        )
        return 0

    lax.fori_loop(1, n * nb, greet, 0)

    gath[0, 0:3, :] = ac_ref[...]
    gath[0, 3:6, :] = an_ref[...]
    gath[0, 6 : 6 + steps, :] = aq_ref[...]

    row = lax.broadcasted_iota(jnp.int32, (steps, width), 0)
    azimuth = jnp.zeros((steps, width), F32)
    for s in range(steps):
        azimuth = jnp.where(row == s, az_ref[s], azimuth)
    angle = azimuth + bi_ref[...].astype(F32) * (math.pi / 2.0)
    cosine = jnp.cos(angle)
    sine = jnp.sin(angle)
    x = bc_ref[:, 0, :]
    y = bc_ref[:, 1, :]
    pos[0] = cosine * x - sine * y
    pos[1] = sine * x + cosine * y
    pos[2] = bc_ref[:, 2, :]
    for s in range(steps):
        strength = bs_ref[s : s + 1, :]
        yparts[s] = split3(
            jnp.concatenate(
                [strength] + [strength * pos[c, s : s + 1, :] for c in range(3)], axis=0
            )
        )
    acc[...] = jnp.zeros_like(acc)

    pl.semaphore_wait(barrier, n * nb - 1)

    def send_frame(k, _):
        other = lax.rem(me_f + n - k, n)
        pltpu.make_async_remote_copy(
            src_ref=gath.at[0],
            dst_ref=gath.at[k],
            send_sem=g_send,
            recv_sem=g_recv.at[k],
            device_id=(other, me_b),
            device_id_type=MESH,
        ).start()
        return 0

    lax.fori_loop(1, n, send_frame, 0)

    for s in range(steps):
        for c in range(3):
            for j in range(width // LANES):
                piece = pos[c, s : s + 1, j * LANES : (j + 1) * LANES]
                spread[s * 3 + c, j * LANES : (j + 1) * LANES, :] = jnp.broadcast_to(
                    piece, (LANES, LANES)
                ).T

    def send_part(k, dest_f, dest_b, chunk):
        pltpu.make_async_remote_copy(
            src_ref=stage.at[k, chunk],
            dst_ref=land.at[k * nb + me_b],
            send_sem=p_send,
            recv_sem=p_recv,
            device_id=(dest_f, dest_b),
            device_id_type=MESH,
        ).start()

    def block(k, _):
        owner = lax.rem(me_f + k, n)

        @pl.when(k > 0)
        def _():
            pltpu.make_async_copy(gath.at[k], gath.at[k], g_recv.at[k]).wait()

        fx = gath[k, 0:1, :]
        fy = gath[k, 1:2, :]
        fz = gath[k, 2:3, :]
        nx = gath[k, 3:4, :]
        ny = gath[k, 4:5, :]
        nz = gath[k, 5:6, :]
        fxb = jnp.broadcast_to(fx, (8, frame))
        fyb = jnp.broadcast_to(fy, (8, frame))
        fzb = jnp.broadcast_to(fz, (8, frame))
        fx16 = jnp.concatenate([fxb, fxb], axis=0)
        fy16 = jnp.concatenate([fyb, fyb], axis=0)
        fz16 = jnp.concatenate([fzb, fzb], axis=0)
        out_rows = []
        for s in range(steps):
            q = gath[k, 6 + s : 7 + s, :]
            xs = split3(jnp.concatenate([q, q * fx, q * fy, q * fz], axis=0))
            slot = s % 2
            for r in range(width // ROWS):
                lines = slice(r * ROWS, (r + 1) * ROWS)
                bx = spread[s * 3, lines, :]
                by = spread[s * 3 + 1, lines, :]
                bz = spread[s * 3 + 2, lines, :]
                for h in range(frame // LANES):
                    cols = slice(h * LANES, (h + 1) * LANES)
                    dx = fx16[:, cols] - bx
                    dy = fy16[:, cols] - by
                    dz = fz16[:, cols] - bz
                    inv = lax.rsqrt(dx * dx + dy * dy + dz * dz + core_sq)
                    weight = inv * inv * inv
                    high = weight.astype(BF16)
                    whi[slot, lines, cols] = high
                    wlo[slot, lines, cols] = (weight - high.astype(F32)).astype(BF16)
            ys = yparts[s]
            high = whi[slot]
            low = wlo[slot]
            sums = fold3(
                jnp.dot(ys, high, preferred_element_type=F32)
                + jnp.dot(ys, low, preferred_element_type=F32)
            )
            base = sums[0:1]
            out_rows.append(
                kernel_scale
                * (
                    nx * (fx * base - sums[1:2])
                    + ny * (fy * base - sums[2:3])
                    + nz * (fz * base - sums[3:4])
                )
            )
            over = (((1,), (1,)), ((), ()))
            acc[s] += lax.dot_general(xs, high, over, preferred_element_type=F32) + lax.dot_general(
                xs, low, over, preferred_element_type=F32
            )
        part = jnp.concatenate(out_rows, axis=0)
        for h in range(frame // LANES):
            stage[k, h] = part[:, h * LANES : (h + 1) * LANES]

        @pl.when(k > 0)
        def _():
            for c in range(nb):
                send_part(k, owner, c, c // per_chunk)

        @pl.when(k == 0)
        def _():
            for d in range(1, nb):
                c = lax.rem(me_b + d, nb)
                send_part(0, me_f, c, c // per_chunk)

        return 0

    lax.fori_loop(0, n, block, 0)

    chunk = me_b // per_chunk
    land[me_b] = stage[0, chunk]

    for s in range(steps):
        sums = fold3(acc[s])
        for c in range(3):
            bv_ref[s, c : c + 1, :] = kernel_scale * (
                pos[c, s : s + 1, :] * sums[0:1] - sums[c + 1 : c + 2]
            )

    own = pl.ds(pl.multiple_of(chunk * LANES, LANES), LANES)
    onset_part = (
        an_ref[0:1, own] * on_ref[0] + an_ref[1:2, own] * on_ref[1] + an_ref[2:3, own] * on_ref[2]
    )
    extra = onset_part + 0.5 * aq_ref[:, own]

    rest = land.at[pl.ds(1, n * nb - 1)]
    pltpu.make_async_copy(rest, rest, p_recv).wait()
    total = jnp.sum(land[...], axis=0)
    resid = total + extra
    which = lax.rem(me_b, per_chunk)
    nv = total[:, 0:quarter]
    rv = resid[:, 0:quarter]
    for i in range(1, per_chunk):
        cols = slice(i * quarter, (i + 1) * quarter)
        nv = jnp.where(which == i, total[:, cols], nv)
        rv = jnp.where(which == i, resid[:, cols], rv)
    nv_ref[...] = nv
    rs_ref[...] = rv

    pltpu.make_async_copy(rest, rest, p_send).wait()
    blocks = gath.at[pl.ds(1, n - 1)]
    pltpu.make_async_copy(blocks, blocks, g_send).wait()


def body(n, nb, ac, an, aq, bc, bs, bi, az, onset):
    steps, _, width = bc.shape
    frame = ac.shape[1]
    quarter = frame // nb
    vmem = pl.BlockSpec(memory_space=pltpu.VMEM)
    smem = pl.BlockSpec(memory_space=pltpu.SMEM)
    return pl.pallas_call(
        functools.partial(kernel, n, nb),
        out_shape=(
            jax.ShapeDtypeStruct((steps, quarter), F32),
            jax.ShapeDtypeStruct((steps, 3, width), F32),
            jax.ShapeDtypeStruct((steps, quarter), F32),
        ),
        in_specs=[vmem] * 6 + [smem] * 2,
        out_specs=(vmem, vmem, vmem),
        scratch_shapes=[
            pltpu.VMEM((n, 16, frame), F32),
            pltpu.VMEM((steps * 3, width, LANES), F32),
            pltpu.VMEM((3, steps, width), F32),
            pltpu.VMEM((steps, 16, width), BF16),
            pltpu.VMEM((16, frame), BF16),
            pltpu.VMEM((2, width, frame), BF16),
            pltpu.VMEM((2, width, frame), BF16),
            pltpu.VMEM((steps, 16, width), F32),
            pltpu.VMEM((n, frame // LANES, steps, LANES), F32),
            pltpu.VMEM((n * nb, steps, LANES), F32),
            pltpu.SemaphoreType.DMA,
            pltpu.SemaphoreType.DMA((n,)),
            pltpu.SemaphoreType.DMA,
            pltpu.SemaphoreType.DMA,
        ],
        compiler_params=pltpu.CompilerParams(
            collective_id=0, has_side_effects=True, vmem_limit_bytes=24 * 1024 * 1024
        ),
    )(ac, an, aq, bc, bs, bi.reshape(1, width), az, onset)


def solution(mesh):
    n = mesh.shape["fus"]
    nb = mesh.shape["blade"]
    both = ("fus", "blade")
    return jax.shard_map(
        functools.partial(body, n, nb),
        mesh=mesh,
        in_specs=(
            P(None, "fus"),
            P(None, "fus"),
            P(None, "fus"),
            P(None, None, both),
            P(None, both),
            P(both),
            P(),
            P(),
        ),
        out_specs=(P(None, both), P(None, None, both), P(None, both)),
        check_vma=False,
    )
```

time: 148 us -> 31.6 us (0.21)
  waiting for transfers between devices: 70 us -> 0 us
  blocking collectives: 32.5 us -> 0 us
  Pallas kernels: 0 us -> 28 us
  other arithmetic: 23.9 us -> 0 us
  between operations: 15.5 us -> 0.76 us
  local copies, waits for them, and re-layouts: 5.46 us -> 2.6 us
    psum x1 -> x0, waiting for transfers between devices: 52.6 us -> none  [body(): totals = lax.psum(blade_term, 'fus')]
    all_gather x1 -> x0, blocking collectives: 32.5 us -> none  [body(): lax.all_gather(packed, 'fus', axis=2, tiled=True)]
    pallas_call x0 -> x1, Pallas kernels: none -> 28 us  [body(): pl.pallas_call(functools.partial(kernel, n, nb), out_shape=(jax.ShapeDtyp...]
    reduce_sum x4 -> x0, other arithmetic: 18.9 us -> none  [tile_terms(): jnp.sum(scaled * delta_x, 0)]
    unnamed x3 -> x0, waiting for transfers between devices: 17.4 us -> none
    add x6 -> x0, other arithmetic: 2.65 us -> none  [the longest x2 2.61 us: body(): residual = normal_velocity + onset_part[None, :] + 0.5 * own_strength]
    dynamic_slice x10 -> x0, local copies, waits for them, and re-layouts: 1.77 us -> none  [the longest x1 1.35 us: body(): lax.dynamic_slice_in_dim(totals, lax.axis_index('fus') * b_rows, b_rows, 2)]
  transfers between devices with their start and end apart: 2 -> 0, of which waited for: 2 -> 0; matrix products, arithmetic and copies ran while one was open for 3% -> 0% of each run, Pallas kernels for 0% -> 0%
where the time goes in v1:
time: 31.6 us; the launch traced here: 31.4 us
  Pallas kernels  28 us (89%)
  local copies, waits for them, and re-layouts  2.6 us (8%)
  between operations  0.76 us (2%)
    pallas_call x1, Pallas kernels, body(): pl.pallas_call(functools.partial(kernel, n, nb), out_shape=(jax.ShapeDtyp...  28 us
    unnamed x17, local copies, waits for them, and re-layouts  1.98 us

profile of v1, /device:TPU:0, one launch (start us, length us, event | category | flops | bytes accessed | tf_op | source)
XLA Modules:
  0.0 31.4 jit_solution(5695677741549677843)
XLA Ops:
  0.6 0.0 copy-start
  0.6 0.0 copy-start.1
  0.7 0.0 copy-start.2
  0.7 0.0 copy-start.3
  0.7 0.0 copy-start.4
  0.7 0.0 copy-start.5
  0.7 0.0 copy-start.6
  0.7 0.8 %copy.11.bc_ref = f32[4,3,512]{2,1,0:T(4,128)S(1)} copy(f32[4,3,512]{2,0,1:T(4,128)} %param.11) | data formatting | bytes 49152 | tf_op args[3]
  1.5 0.0 copy-done
  1.5 0.0 copy-done.1
  1.5 0.0 copy-done.2
  1.5 0.0 copy-done.3
  1.5 0.0 copy-done.4
  1.5 0.0 copy-done.5
  1.6 0.0 copy-done.6
  1.6 28.0 %shard_map.103 = (f32[4,64]{1,0:T(4,128)S(1)}, f32[4,3,512]{2,1,0:T(4,128)S(1)}, f32[4,64]{1,0:T(4,128)S(1)}) custom-call(f32[3,256]{1,0:T(4,128)S(1)} %copy-done.1, f32[3,256]{1,0:T(4,128)S(1)} %copy-done.2, f32[4,256]{1,0:T(4,128)S(1)} %copy-done.3, f32[4,3,512]{2,1,0:T(4,128)S(1)} %copy.11.bc_ref, f32[4,512]{1,0:T(4,128)S(1)} %copy-done, ...), custom_call_target="tpu_custom_call" | custom-call | tf_op jit(solution)/shard_map/pallas_call | solution.py:237
  29.6 0.6 %copy.12 = f32[4,3,512]{2,0,1:T(4,128)} copy(f32[4,3,512]{2,1,0:T(4,128)S(1)} %get-tuple-element.4) | data formatting | bytes 49152 | tf_op jit(solution)/shard_map/pallas_call | solution.py:237
  30.2 0.6 %copy.15 = f32[4,64]{1,0:T(4,128)} copy(f32[4,64]{1,0:T(4,128)S(1)} %get-tuple-element.9) | data formatting | bytes 2048
  30.8 0.6 %copy.16 = f32[4,64]{1,0:T(4,128)} copy(f32[4,64]{1,0:T(4,128)S(1)} %get-tuple-element.11) | data formatting | bytes 2048
Async XLA Ops:
  0.6 0.9 %copy-start = (f32[4,512]{1,0:T(4,128)S(1)}, f32[4,512]{1,0:T(4,128)}, u32[]{:S(2)}) copy-start(f32[4,512]{1,0:T(4,128)} %bs_ref.1) | copy-start | bytes 24580
  0.6 0.9 %copy-start.1 = (f32[3,256]{1,0:T(4,128)S(1)}, f32[3,256]{1,0:T(4,128)}, u32[]{:S(2)}) copy-start(f32[3,256]{1,0:T(4,128)} %ac_ref.1) | copy-start | bytes 9220
  0.7 0.9 %copy-start.2 = (f32[3,256]{1,0:T(4,128)S(1)}, f32[3,256]{1,0:T(4,128)}, u32[]{:S(2)}) copy-start(f32[3,256]{1,0:T(4,128)} %an_ref.1) | copy-start | bytes 9220
  0.7 0.9 %copy-start.3 = (f32[4,256]{1,0:T(4,128)S(1)}, f32[4,256]{1,0:T(4,128)}, u32[]{:S(2)}) copy-start(f32[4,256]{1,0:T(4,128)} %aq_ref.1) | copy-start | bytes 12292
  0.7 0.9 %copy-start.4 = (s32[512]{0:T(512)S(1)}, s32[512]{0:T(512)}, u32[]{:S(2)}) copy-start(s32[512]{0:T(512)} %param.13) | copy-start | bytes 6148
  0.7 0.9 %copy-start.5 = (f32[4]{0:T(128)S(1)}, f32[4]{0:T(128)}, u32[]{:S(2)}) copy-start(f32[4]{0:T(128)} %az_ref.1) | copy-start | bytes 52
  0.7 0.9 %copy-start.6 = (f32[3]{0:T(128)S(1)}, f32[3]{0:T(128)}, u32[]{:S(2)}) copy-start(f32[3]{0:T(128)} %on_ref.1) | copy-start | bytes 40

commit v2 on v1

--- a/solution.py
+++ b/solution.py
@@ -15,6 +15,7 @@
 BF16 = jnp.bfloat16
 LANES = 128
 ROWS = 16
+PIECE = 256
 
 
 def split3(value):
@@ -34,7 +35,7 @@
     n, nb,
     ac_ref, an_ref, aq_ref, bc_ref, bs_ref, bi_ref, az_ref, on_ref,
     nv_ref, bv_ref, rs_ref,
-    gath, spread, pos, yparts, xparts, whi, wlo, acc, stage, land,
+    gath, spread, pos, yparts, acc, stage, land,
     g_send, g_recv, p_send, p_recv,
 ):
     steps = bc_ref.shape[0]
@@ -134,16 +135,25 @@
         fx16 = jnp.concatenate([fxb, fxb], axis=0)
         fy16 = jnp.concatenate([fyb, fyb], axis=0)
         fz16 = jnp.concatenate([fzb, fzb], axis=0)
-        out_rows = []
+        xs = []
         for s in range(steps):
             q = gath[k, 6 + s : 7 + s, :]
-            xs = split3(jnp.concatenate([q, q * fx, q * fy, q * fz], axis=0))
-            slot = s % 2
-            for r in range(width // ROWS):
+            xs.append(split3(jnp.concatenate([q, q * fx, q * fy, q * fz], axis=0)))
+        over = (((1,), (1,)), ((), ()))
+        pieces = [(s, i) for s in range(steps) for i in range(width // PIECE)]
+        held = [[[[] for _ in range(frame // LANES)] for _ in range(2)] for _ in pieces]
+        sums = [None] * steps
+        back = [None] * steps
+
+        def fill(p, part):
+            s, i = pieces[p]
+            each = PIECE // ROWS // 4
+            for r in range(part * each, (part + 1) * each):
                 lines = slice(r * ROWS, (r + 1) * ROWS)
-                bx = spread[s * 3, lines, :]
-                by = spread[s * 3 + 1, lines, :]
-                bz = spread[s * 3 + 2, lines, :]
+                source = slice(i * PIECE + r * ROWS, i * PIECE + (r + 1) * ROWS)
+                bx = spread[s * 3, source, :]
+                by = spread[s * 3 + 1, source, :]
+                bz = spread[s * 3 + 2, source, :]
                 for h in range(frame // LANES):
                     cols = slice(h * LANES, (h + 1) * LANES)
                     dx = fx16[:, cols] - bx
@@ -152,27 +162,42 @@
                     inv = lax.rsqrt(dx * dx + dy * dy + dz * dz + core_sq)
                     weight = inv * inv * inv
                     high = weight.astype(BF16)
-                    whi[slot, lines, cols] = high
-                    wlo[slot, lines, cols] = (weight - high.astype(F32)).astype(BF16)
-            ys = yparts[s]
-            high = whi[slot]
-            low = wlo[slot]
-            sums = fold3(
-                jnp.dot(ys, high, preferred_element_type=F32)
-                + jnp.dot(ys, low, preferred_element_type=F32)
+                    held[p][0][h].append(high)
+                    held[p][1][h].append((weight - high.astype(F32)).astype(BF16))
+
+        def dots(p, part):
+            s, i = pieces[p]
+            source = slice(i * PIECE, (i + 1) * PIECE)
+            weight = jnp.concatenate(
+                [jnp.concatenate(tall, axis=0) for tall in held[p][part % 2]], axis=1
             )
-            base = sums[0:1]
+            if part < 2:
+                term = jnp.dot(yparts[s, :, source], weight, preferred_element_type=F32)
+                sums[s] = term if sums[s] is None else sums[s] + term
+            else:
+                term = lax.dot_general(xs[s], weight, over, preferred_element_type=F32)
+                if part == 2:
+                    back[s] = term
+                else:
+                    acc[s, :, source] += back[s] + term
+
+        for p in range(len(pieces) + 1):
+            for part in range(4):
+                if p < len(pieces):
+                    fill(p, part)
+                if p > 0:
+                    dots(p - 1, part)
+        out_rows = []
+        for s in range(steps):
+            total = fold3(sums[s])
+            base = total[0:1]
             out_rows.append(
                 kernel_scale
                 * (
-                    nx * (fx * base - sums[1:2])
-                    + ny * (fy * base - sums[2:3])
-                    + nz * (fz * base - sums[3:4])
+                    nx * (fx * base - total[1:2])
+                    + ny * (fy * base - total[2:3])
+                    + nz * (fz * base - total[3:4])
                 )
-            )
-            over = (((1,), (1,)), ((), ()))
-            acc[s] += lax.dot_general(xs, high, over, preferred_element_type=F32) + lax.dot_general(
-                xs, low, over, preferred_element_type=F32
             )
         part = jnp.concatenate(out_rows, axis=0)
         for h in range(frame // LANES):
@@ -248,9 +273,6 @@
             pltpu.VMEM((steps * 3, width, LANES), F32),
             pltpu.VMEM((3, steps, width), F32),
             pltpu.VMEM((steps, 16, width), BF16),
-            pltpu.VMEM((16, frame), BF16),
-            pltpu.VMEM((2, width, frame), BF16),
-            pltpu.VMEM((2, width, frame), BF16),
             pltpu.VMEM((steps, 16, width), F32),
             pltpu.VMEM((n, frame // LANES, steps, LANES), F32),
             pltpu.VMEM((n * nb, steps, LANES), F32),

time: 31.6 us -> 26.7 us (0.84)
  Pallas kernels: 28 us -> 23.1 us
    pallas_call x1, Pallas kernels: 28 us -> 23.1 us  [body(): pl.pallas_call(functools.partial(kernel, n, nb), out_shape=(jax.ShapeDtyp...]
where the time goes in v2:
time: 26.7 us; the launch traced here: 26.5 us
  Pallas kernels  23.1 us (87%)
  local copies, waits for them, and re-layouts  2.6 us (10%)
  between operations  0.76 us (3%)
    pallas_call x1, Pallas kernels, body(): pl.pallas_call(functools.partial(kernel, n, nb), out_shape=(jax.ShapeDtyp...  23.1 us
    unnamed x17, local copies, waits for them, and re-layouts  1.98 us
    pallas_call x1, local copies, waits for them, and re-layouts, body(): pl.pallas_call(functools.partial(kernel, n, nb), out_shape=(jax.ShapeDtyp...  0.62 us

profile of v2, /device:TPU:0, one launch (start us, length us, event | category | flops | bytes accessed | tf_op | source)
XLA Modules:
  0.0 26.5 jit_solution(7117005781758814176)
XLA Ops:
  0.6 0.0 copy-start
  0.6 0.0 copy-start.1
  0.7 0.0 copy-start.2
  0.7 0.0 copy-start.3
  0.7 0.0 copy-start.4
  0.7 0.0 copy-start.5
  0.7 0.0 copy-start.6
  0.7 0.8 %copy.11.bc_ref = f32[4,3,512]{2,1,0:T(4,128)S(1)} copy(f32[4,3,512]{2,0,1:T(4,128)} %param.11) | data formatting | bytes 49152 | tf_op args[3]
  1.5 0.0 copy-done
  1.5 0.0 copy-done.1
  1.5 0.0 copy-done.2
  1.5 0.0 copy-done.3
  1.5 0.0 copy-done.4
  1.5 0.0 copy-done.5
  1.6 0.0 copy-done.6
  1.6 23.1 %shard_map.103 = (f32[4,64]{1,0:T(4,128)S(1)}, f32[4,3,512]{2,1,0:T(4,128)S(1)}, f32[4,64]{1,0:T(4,128)S(1)}) custom-call(f32[3,256]{1,0:T(4,128)S(1)} %copy-done.1, f32[3,256]{1,0:T(4,128)S(1)} %copy-done.2, f32[4,256]{1,0:T(4,128)S(1)} %copy-done.3, f32[4,3,512]{2,1,0:T(4,128)S(1)} %copy.11.bc_ref, f32[4,512]{1,0:T(4,128)S(1)} %copy-done, ...), custom_call_target="tpu_custom_call" | custom-call | tf_op jit(solution)/shard_map/pallas_call | solution.py:262
  24.7 0.6 %copy.12 = f32[4,3,512]{2,0,1:T(4,128)} copy(f32[4,3,512]{2,1,0:T(4,128)S(1)} %get-tuple-element.4) | data formatting | bytes 49152 | tf_op jit(solution)/shard_map/pallas_call | solution.py:262
  25.3 0.6 %copy.15 = f32[4,64]{1,0:T(4,128)} copy(f32[4,64]{1,0:T(4,128)S(1)} %get-tuple-element.9) | data formatting | bytes 2048
  25.9 0.6 %copy.16 = f32[4,64]{1,0:T(4,128)} copy(f32[4,64]{1,0:T(4,128)S(1)} %get-tuple-element.11) | data formatting | bytes 2048
Async XLA Ops:
  0.6 0.9 %copy-start = (f32[4,512]{1,0:T(4,128)S(1)}, f32[4,512]{1,0:T(4,128)}, u32[]{:S(2)}) copy-start(f32[4,512]{1,0:T(4,128)} %bs_ref.1) | copy-start | bytes 24580
  0.6 0.9 %copy-start.1 = (f32[3,256]{1,0:T(4,128)S(1)}, f32[3,256]{1,0:T(4,128)}, u32[]{:S(2)}) copy-start(f32[3,256]{1,0:T(4,128)} %ac_ref.1) | copy-start | bytes 9220
  0.7 0.9 %copy-start.2 = (f32[3,256]{1,0:T(4,128)S(1)}, f32[3,256]{1,0:T(4,128)}, u32[]{:S(2)}) copy-start(f32[3,256]{1,0:T(4,128)} %an_ref.1) | copy-start | bytes 9220
  0.7 0.9 %copy-start.3 = (f32[4,256]{1,0:T(4,128)S(1)}, f32[4,256]{1,0:T(4,128)}, u32[]{:S(2)}) copy-start(f32[4,256]{1,0:T(4,128)} %aq_ref.1) | copy-start | bytes 12292
  0.7 0.9 %copy-start.4 = (s32[512]{0:T(512)S(1)}, s32[512]{0:T(512)}, u32[]{:S(2)}) copy-start(s32[512]{0:T(512)} %param.13) | copy-start | bytes 6148
  0.7 0.9 %copy-start.5 = (f32[4]{0:T(128)S(1)}, f32[4]{0:T(128)}, u32[]{:S(2)}) copy-start(f32[4]{0:T(128)} %az_ref.1) | copy-start | bytes 52
  0.7 0.9 %copy-start.6 = (f32[3]{0:T(128)S(1)}, f32[3]{0:T(128)}, u32[]{:S(2)}) copy-start(f32[3]{0:T(128)} %on_ref.1) | copy-start | bytes 40

commit v3 on v2

--- a/solution.py
+++ b/solution.py
@@ -84,8 +84,12 @@
 
     pl.semaphore_wait(barrier, n * nb - 1)
 
+    def offset(k):
+        half = (k + 1) // 2
+        return lax.rem(n + half * (2 * lax.rem(k, 2) - 1), n)
+
     def send_frame(k, _):
-        other = lax.rem(me_f + n - k, n)
+        other = lax.rem(me_f + n - offset(k), n)
         pltpu.make_async_remote_copy(
             src_ref=gath.at[0],
             dst_ref=gath.at[k],
@@ -117,7 +121,7 @@
         ).start()
 
     def block(k, _):
-        owner = lax.rem(me_f + k, n)
+        owner = lax.rem(me_f + offset(k), n)
 
         @pl.when(k > 0)
         def _():

time: 26.7 us -> 26.1 us (0.978)
  Pallas kernels: 23.1 us -> 22.5 us
    pallas_call x1, Pallas kernels: 23.1 us -> 22.5 us  [body(): pl.pallas_call(functools.partial(kernel, n, nb), out_shape=(jax.ShapeDtyp...]
where the time goes in v3:
time: 26.1 us; the launch traced here: 25.8 us
  Pallas kernels  22.5 us (86%)
  local copies, waits for them, and re-layouts  2.6 us (10%)
  between operations  0.76 us (3%)
    pallas_call x1, Pallas kernels, body(): pl.pallas_call(functools.partial(kernel, n, nb), out_shape=(jax.ShapeDtyp...  22.5 us
    unnamed x17, local copies, waits for them, and re-layouts  1.98 us
    pallas_call x1, local copies, waits for them, and re-layouts, body(): pl.pallas_call(functools.partial(kernel, n, nb), out_shape=(jax.ShapeDtyp...  0.62 us

profile of v3, /device:TPU:0, one launch (start us, length us, event | category | flops | bytes accessed | tf_op | source)
XLA Modules:
  0.0 25.8 jit_solution(5475774079277701652)
XLA Ops:
  0.6 0.0 copy-start
  0.6 0.0 copy-start.1
  0.7 0.0 copy-start.2
  0.7 0.0 copy-start.3
  0.7 0.0 copy-start.4
  0.7 0.0 copy-start.5
  0.7 0.0 copy-start.6
  0.7 0.8 %copy.11.bc_ref = f32[4,3,512]{2,1,0:T(4,128)S(1)} copy(f32[4,3,512]{2,0,1:T(4,128)} %param.11) | data formatting | bytes 49152 | tf_op args[3]
  1.5 0.0 copy-done
  1.5 0.0 copy-done.1
  1.5 0.0 copy-done.2
  1.5 0.0 copy-done.3
  1.5 0.0 copy-done.4
  1.5 0.0 copy-done.5
  1.6 0.0 copy-done.6
  1.6 22.5 %shard_map.103 = (f32[4,64]{1,0:T(4,128)S(1)}, f32[4,3,512]{2,1,0:T(4,128)S(1)}, f32[4,64]{1,0:T(4,128)S(1)}) custom-call(f32[3,256]{1,0:T(4,128)S(1)} %copy-done.1, f32[3,256]{1,0:T(4,128)S(1)} %copy-done.2, f32[4,256]{1,0:T(4,128)S(1)} %copy-done.3, f32[4,3,512]{2,1,0:T(4,128)S(1)} %copy.11.bc_ref, f32[4,512]{1,0:T(4,128)S(1)} %copy-done, ...), custom_call_target="tpu_custom_call" | custom-call | tf_op jit(solution)/shard_map/pallas_call | solution.py:266
  24.0 0.6 %copy.12 = f32[4,3,512]{2,0,1:T(4,128)} copy(f32[4,3,512]{2,1,0:T(4,128)S(1)} %get-tuple-element.4) | data formatting | bytes 49152 | tf_op jit(solution)/shard_map/pallas_call | solution.py:266
  24.7 0.6 %copy.15 = f32[4,64]{1,0:T(4,128)} copy(f32[4,64]{1,0:T(4,128)S(1)} %get-tuple-element.9) | data formatting | bytes 2048
  25.2 0.6 %copy.16 = f32[4,64]{1,0:T(4,128)} copy(f32[4,64]{1,0:T(4,128)S(1)} %get-tuple-element.11) | data formatting | bytes 2048
Async XLA Ops:
  0.6 0.9 %copy-start = (f32[4,512]{1,0:T(4,128)S(1)}, f32[4,512]{1,0:T(4,128)}, u32[]{:S(2)}) copy-start(f32[4,512]{1,0:T(4,128)} %bs_ref.1) | copy-start | bytes 24580
  0.6 0.9 %copy-start.1 = (f32[3,256]{1,0:T(4,128)S(1)}, f32[3,256]{1,0:T(4,128)}, u32[]{:S(2)}) copy-start(f32[3,256]{1,0:T(4,128)} %ac_ref.1) | copy-start | bytes 9220
  0.7 0.9 %copy-start.2 = (f32[3,256]{1,0:T(4,128)S(1)}, f32[3,256]{1,0:T(4,128)}, u32[]{:S(2)}) copy-start(f32[3,256]{1,0:T(4,128)} %an_ref.1) | copy-start | bytes 9220
  0.7 0.9 %copy-start.3 = (f32[4,256]{1,0:T(4,128)S(1)}, f32[4,256]{1,0:T(4,128)}, u32[]{:S(2)}) copy-start(f32[4,256]{1,0:T(4,128)} %aq_ref.1) | copy-start | bytes 12292
  0.7 0.9 %copy-start.4 = (s32[512]{0:T(512)S(1)}, s32[512]{0:T(512)}, u32[]{:S(2)}) copy-start(s32[512]{0:T(512)} %param.13) | copy-start | bytes 6148
  0.7 0.9 %copy-start.5 = (f32[4]{0:T(128)S(1)}, f32[4]{0:T(128)}, u32[]{:S(2)}) copy-start(f32[4]{0:T(128)} %az_ref.1) | copy-start | bytes 52
  0.7 0.9 %copy-start.6 = (f32[3]{0:T(128)S(1)}, f32[3]{0:T(128)}, u32[]{:S(2)}) copy-start(f32[3]{0:T(128)} %on_ref.1) | copy-start | bytes 40
